TPU v7x, 32 devices: a whole 2x2x4 slice. The times are simulated.
32 devices in a mesh: freq: 16 (over z, y, x), src: 2 (over core).
Axes of the slice: x: 2, y: 2, z: 4, core: 2. Of those that a mesh axis runs over, the one named last changes fastest.
Arguments:
- samples: bfloat16 [128, 2048, 128], P('freq', None, 'src'), may hold values from -6 to 6
- initial_offset: float32 [2, 1024, 128, 128], P(None, 'freq'), may hold values from -0.875 to 0.875
Outputs:
- demixing: float32 [2, 1024, 128, 128], P(None, 'freq', 'src')
- source_power: float32 [128, 128], P('src')
All inputs are finite; a program needn't handle non-finite values.
Results may differ from a plain program's by a relative error of at most 0.0051.
Values may be sent and summed in bfloat16 or wider, within the bound.
A program may use at most 128 MiB of HBM per device.

v0:
```python
import jax
import jax.numpy as jnp
from jax import lax
from jax.sharding import PartitionSpec as P

ITERS = 3


step_size = 0.3
epsilon = 1e-06


def dft_table(length):
    sample_idx = jnp.arange(length, dtype=jnp.int32)
    bin_idx = jnp.arange(length // 2, dtype=jnp.int32)
    phase = (sample_idx[:, None] * bin_idx[None, :] % length).astype(jnp.float32) * (
        2.0 * jnp.pi / length
    )
    window = (
        0.5 - 0.5 * jnp.cos(sample_idx.astype(jnp.float32) * (2.0 * jnp.pi / length))
    ) * jnp.sqrt(jnp.float32(8.0 / (3.0 * length)))
    return jnp.concatenate(
        [window[:, None] * jnp.cos(phase), -window[:, None] * jnp.sin(phase)], axis=1
    ).astype(jnp.bfloat16)


def batched(left, right, form):
    return jnp.einsum(form, left, right, precision=lax.Precision.HIGHEST)


def demix_rows(w_real, w_imag, x_real, x_imag):
    form = "bkm,bmt->bkt"
    y_real = batched(w_real, x_real, form) - batched(w_imag, x_imag, form)
    y_imag = batched(w_real, x_imag, form) + batched(w_imag, x_real, form)
    return (y_real, y_imag)


def update_rows(
    w_real,
    w_imag,
    own_real,
    own_imag,
    y_real,
    y_imag,
    all_real,
    all_imag,
    source_power,
    identity_rows,
):
    frames = y_real.shape[2]
    phi_real = y_real / source_power
    phi_imag = y_imag / source_power
    form = "bkt,bjt->bkj"
    gram_real = (batched(phi_real, all_real, form) + batched(phi_imag, all_imag, form)) / frames
    gram_imag = (batched(phi_imag, all_real, form) - batched(phi_real, all_imag, form)) / frames
    diff_real = identity_rows - gram_real
    diff_imag = -gram_imag
    other = "bkj,bjm->bkm"
    new_real = own_real + step_size * (
        batched(diff_real, w_real, other) - batched(diff_imag, w_imag, other)
    )
    new_imag = own_imag + step_size * (
        batched(diff_real, w_imag, other) + batched(diff_imag, w_real, other)
    )
    return (new_real, new_imag)


def shards(samples, initial_offset):
    freq_devices = lax.axis_size("freq")
    src_devices = lax.axis_size("src")
    frames_here, length, mics_here = samples.shape
    bin_count = length // 2
    local_bins = initial_offset.shape[1]
    width = initial_offset.shape[2]
    own_count = width // src_devices
    total_bins = local_bins * freq_devices
    frame_total = frames_here * freq_devices
    spectra = jnp.einsum(
        "fnm,nc->cmf", samples, dft_table(length), preferred_element_type=jnp.float32
    ).astype(jnp.bfloat16)
    spectra = spectra.reshape(2, bin_count, mics_here * frames_here)
    regrouped = lax.all_to_all(spectra, "freq", split_axis=1, concat_axis=2, tiled=True)
    regrouped = regrouped.reshape(2, local_bins, freq_devices, mics_here, frames_here)
    regrouped = jnp.transpose(regrouped, (0, 1, 3, 2, 4)).reshape(
        2, local_bins, mics_here, frame_total
    )
    identity = jnp.eye(width, dtype=jnp.float32)
    row_start = lax.axis_index("src") * own_count
    gathered = lax.all_gather(regrouped, "src", axis=2, tiled=True)
    x_real = gathered[0].astype(jnp.float32)
    x_imag = gathered[1].astype(jnp.float32)
    w_real = initial_offset[0] + identity
    w_imag = initial_offset[1]
    identity_rows = lax.dynamic_slice_in_dim(identity, row_start, own_count, 0)
    for sweep in range(ITERS):
        own_real = lax.dynamic_slice_in_dim(w_real, row_start, own_count, 1)
        own_imag = lax.dynamic_slice_in_dim(w_imag, row_start, own_count, 1)
        y_real, y_imag = demix_rows(own_real, own_imag, x_real, x_imag)
        rounded = lax.optimization_barrier(jnp.stack([y_real, y_imag]).astype(jnp.bfloat16))
        values = rounded.astype(jnp.float32)
        bin_sums = jnp.sum(values[0] * values[0] + values[1] * values[1], axis=0)
        summed = lax.psum(bin_sums, "freq")
        source_power = jnp.sqrt(summed / total_bins + epsilon)
        every_source = lax.all_gather(rounded, "src", axis=2, tiled=True).astype(jnp.float32)
        new_real, new_imag = update_rows(
            w_real,
            w_imag,
            own_real,
            own_imag,
            values[0],
            values[1],
            every_source[0],
            every_source[1],
            source_power,
            identity_rows,
        )
        if sweep + 1 < ITERS:
            both_parts = lax.all_gather(jnp.stack([new_real, new_imag]), "src", axis=2, tiled=True)
            w_real, w_imag = (both_parts[0], both_parts[1])
    return (jnp.stack([new_real, new_imag]), source_power)


def solution(mesh):
    in_specs = (P("freq", None, "src"), P(None, "freq", None, None))
    out_specs = (P(None, "freq", "src", None), P("src", None))
    return jax.shard_map(shards, mesh=mesh, in_specs=in_specs, out_specs=out_specs, check_vma=False)
```

profile of v0, /device:TPU:0, one launch (start us, length us, event | category | flops | bytes accessed | tf_op | source)
XLA Modules:
  0.0 586.7 jit_solution(266473079987235918)
XLA Ops:
  7.3 34.8 %multiply_convert_fusion = (bf16[2048,1024]{1,0:T(8,128)(2,1)S(1)}, bf16[2048,1024]{1,0:T(8,128)(2,1)S(1)}) fusion(f32[2048]{0:T(1024)S(1)} %fusion.142, f32[2048]{0:T(1024)S(1)} %subtract_multiply_fusion), kind=kLoop, calls=%fused_computation.10 | loop fusion | flops 37748736 | bytes 8404992 | tf_op jit(solution)/shard_map/convert.13
  42.1 4.6 fusion.3
  47.0 2.5 copy.19
  49.5 3.3 reshape.44
  52.8 5.9 %copy.20 = bf16[2,1024,512]{2,0,1:T(2,128)(2,1)} copy(bf16[2,1024,512]{1,0,2:T(2,128)(2,1)S(1)} %reshape.44) | data formatting | bytes 4194304 | tf_op jit(solution)/shard_map/reshape | solution.py:81
  58.7 57.2 %all_to_all.15 = bf16[2,1024,512]{2,0,1:T(2,128)(2,1)S(1)} all-to-all(bf16[2,1024,512]{2,0,1:T(2,128)(2,1)} %copy.20), channel_id=1, replica_groups=mesh['freq'=16,'src'=2] {'freq'}, dimensions={1} | all-to-all | bytes 4194304 | tf_op jit(solution)/shard_map/all_to_all | solution.py:82
  116.2 3.1 copy.22
  119.3 8.1 %copy.23 = bf16[2,64,64,16,8]{2,4,3,1,0:T(8,128)(2,1)} copy(bf16[2,64,64,16,8]{1,4,2,3,0:T(8,128)(2,1)} %bitcast.256) | data formatting | bytes 4194304 | tf_op jit(solution)/shard_map/transpose | solution.py:84
  127.4 4.8 copy.24
  132.5 4.7 slice.74
  137.2 5.4 bitcast_add_fusion
  144.3 4.2 fusion.50
  148.5 3.6 fusion.52
  161.8 77.4 %psum.21 = f32[64,128]{1,0:T(8,128)S(1)} all-reduce(f32[64,128]{1,0:T(8,128)S(1)} %add_reduce_fusion.2), channel_id=1, replica_groups=mesh['freq'=16,'src'=2] {'freq'}, use_global_device_ids=true, to_apply=%region_1.2 | all-reduce | flops 8192 | bytes 65536 | tf_op jit(solution)/shard_map/psum | solution.py:102
  239.2 6.6 %fusion.61 = f32[64,64,128]{2,1,0:T(8,128)S(1)} fusion(bf16[2,64,128,128]{3,2,1,0:T(8,128)(2,1)} %all-gather.9.cloned.1.call-done, f32[2,64,64,128]{3,2,1,0:T(8,128)} %copy-done.21, f32[64,128]{1,0:T(8,128)S(1)} %add_sqrt_fusion.2), kind=kOutput, calls=%fused_computation.109 | convolution fusion | flops 805830656 | bytes 6324224 | tf_op jit(solution)/shard_map/bkt,bjt->bkj/dot_general | solution.py:28
  245.8 4.2 multiply_negate_fusion.2
  250.1 4.2 fusion.166
  254.2 4.2 fusion.62
  258.4 4.4 multiply_subtract_fusion.2
  262.9 4.1 fusion.165
  267.0 4.2 fusion.54
  271.3 4.4 add_bitcast_fusion
  275.7 2.5 pad_maximum_fusion
  278.3 15.8 %all-gather.11.cloned.1.call-done = f32[2,64,128,128]{3,2,1,0:T(8,128)} async-done(((f32[2,64,64,128]{3,2,1,0:T(8,128)}), f32[2,64,128,128]{3,2,1,0:T(8,128)}) %all-gather.11.cloned.1.call-update) | async-done | bytes 8388624 | tf_op jit(solution)/shard_map/all_gather | solution.py:118
  294.2 4.2 fusion.164
  309.9 2.0 copy-done.23
  312.2 77.4 %psum.22 = f32[64,128]{1,0:T(8,128)S(1)} all-reduce(f32[64,128]{1,0:T(8,128)S(1)} %add_reduce_fusion.1), channel_id=1, replica_groups=mesh['freq'=16,'src'=2] {'freq'}, use_global_device_ids=true, to_apply=%region_3.4 | all-reduce | flops 8192 | bytes 65536 | tf_op jit(solution)/shard_map/psum | solution.py:102
  389.7 6.6 %fusion.65 = f32[64,64,128]{2,1,0:T(8,128)S(1)} fusion(bf16[2,64,128,128]{3,2,1,0:T(8,128)(2,1)} %all-gather.13.cloned.1.call-done, f32[2,64,64,128]{3,2,1,0:T(8,128)} %copy-done.23, f32[64,128]{1,0:T(8,128)S(1)} %add_sqrt_fusion.1), kind=kOutput, calls=%fused_computation.113 | convolution fusion | flops 805830656 | bytes 6324224 | tf_op jit(solution)/shard_map/bkt,bjt->bkj/dot_general | solution.py:28
  396.3 4.3 fusion.66
  400.5 4.3 multiply_negate_fusion.1
  404.9 4.2 fusion.20
  409.1 4.5 multiply_subtract_fusion.1
  413.5 4.2 fusion.49
  417.8 4.1 fusion.18
  421.9 4.4 fusion.44
  426.4 2.5 pad_maximum_fusion.1
  429.0 15.8 %all-gather.15.cloned.1.call-done = f32[2,64,128,128]{3,2,1,0:T(8,128)} async-done(((f32[2,64,64,128]{3,2,1,0:T(8,128)}), f32[2,64,128,128]{3,2,1,0:T(8,128)}) %all-gather.15.cloned.1.call-update) | async-done | bytes 8388624 | tf_op jit(solution)/shard_map/all_gather | solution.py:118
  444.8 4.2 fusion.163
  462.9 77.4 %psum.23 = f32[64,128]{1,0:T(8,128)S(1)} all-reduce(f32[64,128]{1,0:T(8,128)S(1)} %add_reduce_fusion), channel_id=1, replica_groups=mesh['freq'=16,'src'=2] {'freq'}, use_global_device_ids=true, to_apply=%region_5.6 | all-reduce | flops 8192 | bytes 65536 | tf_op jit(solution)/shard_map/psum | solution.py:102
  540.4 6.6 %fusion.69 = f32[64,64,128]{2,1,0:T(8,128)S(1)} fusion(bf16[2,64,128,128]{3,2,1,0:T(8,128)(2,1)} %all-gather.17.cloned.1.call-done, f32[2,64,64,128]{3,2,1,0:T(8,128)} %copy-done.19, f32[64,128]{1,0:T(8,128)S(1)} %add_sqrt_fusion), kind=kOutput, calls=%fused_computation.117 | convolution fusion | flops 805830656 | bytes 6324224 | tf_op jit(solution)/shard_map/bkt,bjt->bkj/dot_general | solution.py:28
  547.0 4.3 fusion.70
  551.2 4.3 multiply_negate_fusion
  555.6 4.2 fusion.12
  559.8 4.5 multiply_subtract_fusion
  564.3 4.2 fusion.39
  568.5 4.1 fusion.10
  572.6 4.4 fusion.34
  577.1 2.5 pad_maximum_fusion.2
  (116 shorter events, 38.3 us)
Async XLA Ops:
  7.2 34.9 %copy-start = (bf16[8,2048,64]{1,2,0:T(8,128)(2,1)S(1)}, bf16[8,2048,64]{1,2,0:T(8,128)(2,1)}, u32[]{:S(2)}) copy-start(bf16[8,2048,64]{1,2,0:T(8,128)(2,1)} %param.2) | copy-start | bytes 6291460
  7.2 137.1 %all-gather.7.cloned.1.call-start = ((), (), s32[]{:S(2)}) async-start(), calls=%async_computation.1 | async-start | bytes 6291456 | tf_op jit(solution)/shard_map/all_gather | solution.py:89
  132.2 107.0 %all-gather.9.cloned.1.call-start = ((), (), s32[]{:S(2)}) async-start(), calls=%async_computation.2 | async-start | bytes 6291456 | tf_op jit(solution)/shard_map/all_gather | solution.py:104
  144.3 4.2 copy-start.2
  148.5 3.6 copy-start.5
  157.5 1.6 copy-start.16
  157.5 136.7 %all-gather.11.cloned.1.call-start = ((), (), s32[]{:S(2)}) async-start(), calls=%async_computation.3 | async-start | bytes 12582912 | tf_op jit(solution)/shard_map/all_gather | solution.py:118
  159.5 1.9 copy-start.21
  239.2 6.6 %copy-start.22 = (f32[2,64,64,128]{3,2,1,0:T(8,128)S(1)}, f32[2,64,64,128]{3,2,1,0:T(8,128)}, u32[]{:S(2)}) copy-start(f32[2,64,64,128]{3,2,1,0:T(8,128)} %copy-done.21) | copy-start | bytes 12582916
  239.2 6.6 %copy-start.26 = (bf16[2,64,128,128]{3,2,1,0:T(8,128)(2,1)S(1)}, bf16[2,64,128,128]{3,2,1,0:T(8,128)(2,1)}, u32[]{:S(2)}) copy-start(bf16[2,64,128,128]{3,2,1,0:T(8,128)(2,1)} %all-gather.9.cloned.1.call-done) | copy-start | bytes 12582916
  245.8 4.2 copy-start.6
  258.4 12.8 %slice-start.4 = ((s8[8388608]{0:T(1024)(128)(4,1)}), s8[4194304]{0:T(1024)(128)(4,1)S(1)}, s32[]{:S(2)}) async-start(s8[8388608]{0:T(1024)(128)(4,1)} %bitcast.254), calls=%async_computation.11 | async-start | bytes 8388608
  262.8 4.2 copy-start.7
  262.9 8.4 %slice-start.5 = ((s8[8388608]{0:T(1024)(128)(4,1)}), s8[4194304]{0:T(1024)(128)(4,1)S(1)}, s32[]{:S(2)}) async-start(s8[8388608]{0:T(1024)(128)(4,1)} %bitcast.254), calls=%async_computation.12 | async-start | bytes 8388608
  278.3 111.4 %all-gather.13.cloned.1.call-start = ((), (), s32[]{:S(2)}) async-start(), calls=%async_computation.4 | async-start | bytes 6291456 | tf_op jit(solution)/shard_map/all_gather | solution.py:104
  294.2 4.6 copy-start.3
  298.4 4.1 copy-start.12
  298.4 6.0 %copy-start.8 = (f32[1,64,128,128]{3,2,1,0:T(8,128)}, f32[1,64,128,128]{3,2,1,0:T(8,128)S(1)}, u32[]{:S(2)}) copy-start(f32[1,64,128,128]{3,2,1,0:T(8,128)S(1)} %get-tuple-element.4) | copy-start | bytes 12582916
  307.8 1.6 copy-start.17
  307.9 136.9 %all-gather.15.cloned.1.call-start = ((), (), s32[]{:S(2)}) async-start(), calls=%async_computation.5 | async-start | bytes 12582912 | tf_op jit(solution)/shard_map/all_gather | solution.py:118
  309.9 2.0 copy-start.23
  389.7 6.6 %copy-start.24 = (f32[2,64,64,128]{3,2,1,0:T(8,128)S(1)}, f32[2,64,64,128]{3,2,1,0:T(8,128)}, u32[]{:S(2)}) copy-start(f32[2,64,64,128]{3,2,1,0:T(8,128)} %copy-done.23) | copy-start | bytes 12582916
  389.7 6.6 %copy-start.27 = (bf16[2,64,128,128]{3,2,1,0:T(8,128)(2,1)S(1)}, bf16[2,64,128,128]{3,2,1,0:T(8,128)(2,1)}, u32[]{:S(2)}) copy-start(bf16[2,64,128,128]{3,2,1,0:T(8,128)(2,1)} %all-gather.13.cloned.1.call-done) | copy-start | bytes 12582916
  396.3 8.6 %slice-start = ((s8[8388608]{0:T(1024)(128)(4,1)}), s8[4194304]{0:T(1024)(128)(4,1)S(1)}, s32[]{:S(2)}) async-start(s8[8388608]{0:T(1024)(128)(4,1)} %bitcast.250), calls=%async_computation.7 | async-start | bytes 8388608
  400.5 4.3 slice-start.1
  409.1 4.5 copy-start.9
  417.8 4.2 copy-start.13
  428.9 111.4 %all-gather.17.cloned.1.call-start = ((), (), s32[]{:S(2)}) async-start(), calls=%async_computation.6 | async-start | bytes 6291456 | tf_op jit(solution)/shard_map/all_gather | solution.py:104
  444.8 4.6 copy-start.4
  449.0 4.1 copy-start.14
  449.0 6.0 %copy-start.10 = (f32[1,64,128,128]{3,2,1,0:T(8,128)}, f32[1,64,128,128]{3,2,1,0:T(8,128)S(1)}, u32[]{:S(2)}) copy-start(f32[1,64,128,128]{3,2,1,0:T(8,128)S(1)} %get-tuple-element.2) | copy-start | bytes 12582916
  458.5 1.6 copy-start.18
  460.6 2.0 copy-start.19
  540.3 19.4 %copy-start.25 = (f32[64,128]{1,0:T(8,128)}, f32[64,128]{1,0:T(8,128)S(1)}, u32[]{:S(2)}) copy-start(f32[64,128]{1,0:T(8,128)S(1)} %add_sqrt_fusion) | copy-start | bytes 98308
  540.4 6.6 %copy-start.20 = (f32[2,64,64,128]{3,2,1,0:T(8,128)S(1)}, f32[2,64,64,128]{3,2,1,0:T(8,128)}, u32[]{:S(2)}) copy-start(f32[2,64,64,128]{3,2,1,0:T(8,128)} %copy-done.19) | copy-start | bytes 12582916
  540.4 6.6 %copy-start.28 = (bf16[2,64,128,128]{3,2,1,0:T(8,128)(2,1)S(1)}, bf16[2,64,128,128]{3,2,1,0:T(8,128)(2,1)}, u32[]{:S(2)}) copy-start(bf16[2,64,128,128]{3,2,1,0:T(8,128)(2,1)} %all-gather.17.cloned.1.call-done) | copy-start | bytes 12582916
  547.0 8.6 %slice-start.2 = ((s8[8388608]{0:T(1024)(128)(4,1)}), s8[4194304]{0:T(1024)(128)(4,1)S(1)}, s32[]{:S(2)}) async-start(s8[8388608]{0:T(1024)(128)(4,1)} %bitcast.252), calls=%async_computation.9 | async-start | bytes 8388608
  551.2 4.3 slice-start.3
  559.8 4.5 copy-start.11
  568.5 4.1 copy-start.15
  577.1 2.6 copy-start.1
Sparse Core Ops, SparseCore 0:
  132.3 11.9 all-gather.6
  157.6 14.8 all-gather.8
  278.4 15.7 all-gather.10
  308.0 14.8 all-gather.12
  429.0 15.7 all-gather.14
  458.7 14.8 all-gather.16
where the time goes:
time: 595 us; the launch traced here: 587 us
  blocking collectives  289 us (49%)
  matrix products  140 us (24%)
  other arithmetic  55.1 us (9%)
  local copies, waits for them, and re-layouts  52.6 us (9%)
  waiting for transfers between devices  33.6 us (6%)
  between operations  15.2 us (3%)
    psum x3, blocking collectives, shards(): summed = lax.psum(bin_sums, 'freq')  232 us
    dot_general x36, matrix products, batched(): return jnp.einsum(form, left, right, precision=lax.Precision.HIGHEST)  136 us
    all_to_all x1, blocking collectives, shards(): lax.all_to_all(spectra, 'freq', split_axis=1, concat_axis=2, tiled=True)  57.2 us
    another operation x1, other arithmetic  34.8 us
    all_gather x2, waiting for transfers between devices, shards(): lax.all_gather(jnp.stack([new_real, new_imag]), 'src', axis=2, tiled=True)  31.7 us
  transfers between devices with their start and end apart: 6, of which 3 were waited for; matrix products, arithmetic and copies ran while one was open for 2% of the time, Pallas kernels for 0%

commit v1 on v0

v1 whole, which is shorter than its diff:
```python
import functools

import jax
import jax.numpy as jnp
from jax import lax
from jax.experimental import pallas as pl
from jax.experimental.pallas import tpu as pltpu
from jax.sharding import PartitionSpec as P

ITERS = 3

step_size = 0.3
epsilon = 1e-06
MESH = pl.DeviceIdType.MESH
LOW_STEPS = 64


def waves(count, stride, length):
    index = jnp.arange(count, dtype=jnp.int32) * stride
    bin_idx = jnp.arange(length // 2, dtype=jnp.int32)
    phase = (index[:, None] * bin_idx[None, :] % length).astype(jnp.float32) * (
        2.0 * jnp.pi / length
    )
    return lax.optimization_barrier((jnp.cos(phase), jnp.sin(phase)))


def dft_table(length):
    high_cos, high_sin = waves(length // LOW_STEPS, LOW_STEPS, length)
    low_cos, low_sin = waves(LOW_STEPS, 1, length)
    sample_idx = jnp.arange(length, dtype=jnp.int32)
    window = (
        0.5 - 0.5 * jnp.cos(sample_idx.astype(jnp.float32) * (2.0 * jnp.pi / length))
    ) * jnp.sqrt(jnp.float32(8.0 / (3.0 * length)))
    window = lax.optimization_barrier(window).reshape(-1, LOW_STEPS, 1)
    a_cos, a_sin = high_cos[:, None, :], high_sin[:, None, :]
    b_cos, b_sin = low_cos[None], low_sin[None]
    cos_part = (window * (a_cos * b_cos - a_sin * b_sin)).astype(jnp.bfloat16)
    sin_part = (-window * (a_sin * b_cos + a_cos * b_sin)).astype(jnp.bfloat16)
    return jnp.concatenate([cos_part, sin_part], axis=2).reshape(length, length)


def halves(value):
    high = value.astype(jnp.bfloat16)
    low = (value - high.astype(jnp.float32)).astype(jnp.bfloat16)
    return high, low


def dot_nn(left, right):
    return lax.dot_general(left, right, (((1,), (0,)), ((), ())), preferred_element_type=jnp.float32)


def dot_nt(left, right):
    return lax.dot_general(left, right, (((1,), (1,)), ((), ())), preferred_element_type=jnp.float32)


def block_pair(real_imag, width):
    swapped = jnp.concatenate([-real_imag[:, width:], real_imag[:, :width]], axis=1)
    return jnp.concatenate([real_imag, swapped], axis=0)


def demix_kernel(
    dims,
    x_ref,
    offset_ref,
    out_ref,
    power_ref,
    stage,
    w_buf,
    x_buf,
    y_buf,
    sums,
    power,
    parts,
    received,
    gathered,
    load_sem,
    send_sem,
    recv_sem,
    last_sem,
):
    freq_devices, src_devices, total_bins = dims
    devices = freq_devices * src_devices
    my_freq, my_src = lax.axis_index("freq"), lax.axis_index("src")
    me = my_freq * src_devices + my_src
    bins, frames, width = x_ref.shape[1], x_ref.shape[2], x_ref.shape[3]
    rows = width // src_devices
    chunk = width // devices

    def place(index):
        return (index // src_devices, lax.rem(index, src_devices))

    load = pltpu.make_async_copy(
        offset_ref.at[:, pl.ds(my_src * bins, bins)], stage, load_sem
    )
    load.start()

    barrier = pltpu.get_barrier_semaphore()

    def greet(step, carry):
        pl.semaphore_signal(
            barrier, inc=1, device_id=place(lax.rem(me + step, devices)), device_id_type=MESH
        )
        return carry

    lax.fori_loop(1, devices, greet, 0)
    load.wait()
    row_id = lax.broadcasted_iota(jnp.int32, (width, 2 * width), 0)
    col_id = lax.broadcasted_iota(jnp.int32, (width, 2 * width), 1)
    identity = jnp.where(row_id == col_id, 1.0, 0.0).astype(jnp.float32)

    def separate(b, w):
        high, low = halves(w)
        product = dot_nt(jnp.concatenate([high, low], axis=0), x_buf[b])
        y = (product[:width] + product[width:]).astype(jnp.bfloat16)
        y_buf[b] = y
        values = y.astype(jnp.float32)
        squares = values * values
        sums[...] += squares[:, :frames] + squares[:, frames:]

    def first(b, carry):
        w = jnp.concatenate([stage[0, b], stage[1, b]], axis=1) + identity
        w_buf[b] = w
        x_real, x_imag = x_ref[0, b], x_ref[1, b]
        upper = jnp.concatenate([x_real, -x_imag], axis=1)
        lower = jnp.concatenate([x_imag, x_real], axis=1)
        x_buf[b] = jnp.concatenate([upper, lower], axis=0)
        separate(b, w)
        return carry

    def improved(b, scale):
        y = y_buf[b]
        high, low = halves(y.astype(jnp.float32) * scale)
        product = dot_nt(jnp.concatenate([high, low], axis=0), block_pair(y, frames))
        diff = identity - (product[:width] + product[width:])
        d_high, d_low = halves(diff)
        w = w_buf[b]
        w_high, w_low = halves(w)
        change = dot_nn(jnp.concatenate([d_high, d_low], axis=0), block_pair(w_high, width))
        change_low = dot_nn(d_high, block_pair(w_low, width))
        return w + step_size * (change[:width] + change[width:] + change_low)

    def add_up(sweep):
        total = sums[...]
        for owner in range(devices):
            parts[owner] = total[owner * chunk : (owner + 1) * chunk]

        def scatter(step, carry):
            owner = lax.rem(me + step, devices)
            pltpu.make_async_remote_copy(
                src_ref=parts.at[owner],
                dst_ref=received.at[sweep, step - 1],
                send_sem=send_sem.at[sweep, 0],
                recv_sem=recv_sem.at[sweep, 0],
                device_id=place(owner),
                device_id_type=MESH,
            ).start()
            return carry

        lax.fori_loop(1, devices, scatter, 0)
        pltpu.make_async_copy(
            received.at[sweep], received.at[sweep], recv_sem.at[sweep, 0]
        ).wait()
        mine = parts[me] + jnp.sum(received[sweep], axis=0)
        gathered[sweep, me] = jnp.sqrt(mine / total_bins + epsilon)

        def spread(step, carry):
            pltpu.make_async_remote_copy(
                src_ref=gathered.at[sweep, me],
                dst_ref=gathered.at[sweep, me],
                send_sem=send_sem.at[sweep, 1],
                recv_sem=recv_sem.at[sweep, 1],
                device_id=place(lax.rem(me + step, devices)),
                device_id_type=MESH,
            ).start()
            return carry

        lax.fori_loop(1, devices, spread, 0)
        for phase in range(2):
            pltpu.make_async_copy(
                received.at[sweep], received.at[sweep], send_sem.at[sweep, phase]
            ).wait()
        pltpu.make_async_copy(
            received.at[sweep], received.at[sweep], recv_sem.at[sweep, 1]
        ).wait()
        for owner in range(devices):
            power[owner * chunk : (owner + 1) * chunk] = gathered[sweep, owner]
        inverse = 1.0 / (power[...] * frames)
        return jnp.concatenate([inverse, inverse], axis=1)

    sums[...] = jnp.zeros_like(sums)
    lax.fori_loop(0, bins, first, 0)
    pl.semaphore_wait(barrier, devices - 1)

    for sweep in range(ITERS - 1):
        scale = add_up(sweep)
        sums[...] = jnp.zeros_like(sums)

        def again(b, carry, scale=scale):
            w = improved(b, scale)
            w_buf[b] = w
            separate(b, w)
            return carry

        lax.fori_loop(0, bins, again, 0)

    scale = add_up(ITERS - 1)
    power_ref[...] = power[pl.ds(pl.multiple_of(my_src * rows, rows), rows), :]

    def last(b, carry):
        w = improved(b, scale)
        stage[0, b] = w[:, :width]
        stage[1, b] = w[:, width:]
        return carry

    lax.fori_loop(0, bins, last, 0)
    here = pl.ds(my_src * bins, bins)
    keep = pltpu.make_async_copy(
        stage.at[:, :, pl.ds(pl.multiple_of(my_src * rows, rows), rows)],
        out_ref.at[:, here],
        load_sem,
    )
    keep.start()
    other = 1 - my_src
    give = pltpu.make_async_remote_copy(
        src_ref=stage.at[:, :, pl.ds(pl.multiple_of(other * rows, rows), rows)],
        dst_ref=out_ref.at[:, here],
        send_sem=last_sem.at[0],
        recv_sem=last_sem.at[1],
        device_id=(my_freq, other),
        device_id_type=MESH,
    )
    give.start()
    keep.wait()
    give.wait()


def shards(samples, initial_offset):
    freq_devices = lax.axis_size("freq")
    src_devices = lax.axis_size("src")
    devices = freq_devices * src_devices
    frames_here, length, mics_here = samples.shape
    bin_count = length // 2
    pair_bins = initial_offset.shape[1]
    bins = pair_bins // src_devices
    width = initial_offset.shape[2]
    frame_total = frames_here * freq_devices
    chunk = width // devices
    spectra = jnp.einsum(
        "fnm,nc->cfm", samples, dft_table(length), preferred_element_type=jnp.float32
    ).astype(jnp.bfloat16)
    spectra = spectra.reshape(2, bin_count, frames_here * mics_here)
    regrouped = lax.all_to_all(
        spectra, ("freq", "src"), split_axis=1, concat_axis=2, tiled=True
    )
    regrouped = regrouped.reshape(
        2, bins, freq_devices, src_devices, frames_here, mics_here
    )
    x = jnp.transpose(regrouped, (0, 1, 2, 4, 3, 5)).reshape(2, bins, frame_total, width)
    f32, bf16 = jnp.float32, jnp.bfloat16
    return pl.pallas_call(
        functools.partial(demix_kernel, (freq_devices, src_devices, bin_count)),
        out_shape=(
            jax.ShapeDtypeStruct((2, pair_bins, width // src_devices, width), f32),
            jax.ShapeDtypeStruct((width // src_devices, frame_total), f32),
        ),
        in_specs=[
            pl.BlockSpec(memory_space=pltpu.VMEM),
            pl.BlockSpec(memory_space=pl.ANY),
        ],
        out_specs=(
            pl.BlockSpec(memory_space=pl.ANY),
            pl.BlockSpec(memory_space=pltpu.VMEM),
        ),
        scratch_shapes=[
            pltpu.VMEM((2, bins, width, width), f32),
            pltpu.VMEM((bins, width, 2 * width), f32),
            pltpu.VMEM((bins, 2 * frame_total, 2 * width), bf16),
            pltpu.VMEM((bins, width, 2 * frame_total), bf16),
            pltpu.VMEM((width, frame_total), f32),
            pltpu.VMEM((width, frame_total), f32),
            pltpu.VMEM((devices, chunk, frame_total), f32),
            pltpu.VMEM((ITERS, devices - 1, chunk, frame_total), f32),
            pltpu.VMEM((ITERS, devices, chunk, frame_total), f32),
            pltpu.SemaphoreType.DMA,
            pltpu.SemaphoreType.DMA((ITERS, 2)),
            pltpu.SemaphoreType.DMA((ITERS, 2)),
            pltpu.SemaphoreType.DMA((2,)),
        ],
        compiler_params=pltpu.CompilerParams(
            collective_id=0, has_side_effects=True, vmem_limit_bytes=48 * 1024 * 1024
        ),
    )(x, initial_offset)


def solution(mesh):
    in_specs = (P("freq", None, "src"), P(None, "freq", None, None))
    out_specs = (P(None, "freq", "src", None), P("src", None))
    return jax.shard_map(shards, mesh=mesh, in_specs=in_specs, out_specs=out_specs, check_vma=False)
```

time: 595 us -> 205 us (0.34); the launches traced: 587 us -> 205 us
  blocking collectives: 289 us -> 55.8 us
  matrix products: 140 us -> 4.58 us
  Pallas kernels: 0 us -> 94.1 us
  other arithmetic: 55.1 us -> 7.53 us
  waiting for transfers between devices: 33.6 us -> 0 us
  between operations: 15.2 us -> 0.72 us
  local copies, waits for them, and re-layouts: 52.6 us -> 42 us
    psum x3 -> x0, blocking collectives: 232 us -> none  [shards(): summed = lax.psum(bin_sums, 'freq')]
    dot_general x36 -> x0, matrix products: 136 us -> none  [batched(): return jnp.einsum(form, left, right, precision=lax.Precision.HIGHEST)]
    pallas_call x0 -> x1, Pallas kernels: none -> 94.1 us  [shards(): pl.pallas_call(functools.partial(demix_kernel, (freq_devices, src_devices...]
    another operation x7 -> x0, other arithmetic: 47 us -> none
    all_gather x6 -> x0, waiting for transfers between devices: 33.5 us -> none  [the longest x2 31.7 us: shards(): lax.all_gather(jnp.stack([new_real, new_imag]), 'src', axis=2, tiled=True)]
    slice x3 -> x0, local copies, waits for them, and re-layouts: 13.1 us -> none  [the longest x2 8.39 us: shards(): w_real, w_imag = (both_parts[0], both_parts[1])]
    reshape x3 -> x4, local copies, waits for them, and re-layouts: 13.9 us -> 22.6 us  [the longest x2 11.1 us: shards(): spectra = spectra.reshape(2, bin_count, frames_here * mics_here)]
  transfers between devices with their start and end apart: 6 -> 0, of which waited for: 3 -> 0; matrix products, arithmetic and copies ran while one was open for 2% -> 0% of each run, Pallas kernels for 0% -> 0%
where the time goes in v1:
time: 205 us
  Pallas kernels  94.1 us (46%)
  blocking collectives  55.8 us (27%)
  local copies, waits for them, and re-layouts  42 us (20%)
  other arithmetic  7.53 us (4%)
  matrix products  4.58 us (2%)
    pallas_call x1, Pallas kernels, shards(): pl.pallas_call(functools.partial(demix_kernel, (freq_devices, src_devices...  94.1 us
    all_to_all x1, blocking collectives, shards(): lax.all_to_all(spectra, ('freq', 'src'), split_axis=1, concat_axis=2, til...  55.8 us
    reshape x2, local copies, waits for them, and re-layouts, shards(): spectra = spectra.reshape(2, bin_count, frames_here * mics_here)  11.1 us
    transpose x1, local copies, waits for them, and re-layouts, shards(): jnp.transpose(regrouped, (0, 1, 2, 4, 3, 5))  9.22 us
    unnamed x10, local copies, waits for them, and re-layouts  8.66 us
    reshape x1, local copies, waits for them, and re-layouts, shards(): jnp.transpose(regrouped, (0, 1, 2, 4, 3, 5))  7.93 us
    unnamed x1, matrix products  4.58 us

profile of v1, /device:TPU:0, one launch (start us, length us, event | category | flops | bytes accessed | tf_op | source)
XLA Modules:
  0.0 204.7 jit_solution(2342650495441584541)
XLA Ops:
  0.6 0.0 copy-start
  0.7 0.1 subtract_multiply_fusion
  0.7 1.0 fusion.15
  1.8 0.6 fusion.20
  2.4 2.5 %multiply_subtract_fusion = (f32[32,64,1024]{2,1,0:T(8,128)S(1)}, f32[32,64,1024]{2,1,0:T(8,128)S(1)}) fusion(f32[64,1024]{1,0:T(8,128)S(1)} %get-tuple-element.9, f32[32,1024]{1,0:T(8,128)S(1)} %get-tuple-element.8, f32[64,1024]{1,0:T(8,128)S(1)} %get-tuple-element.7, f32[32,1024]{1,0:T(8,128)S(1)} %get-tuple-element.6), kind=kLoop, calls=%fused_computation.9 | loop fusion | flops 12582912 | bytes 17563648 | tf_op jit(solution)/shard_map/sub | solution.py:37
  4.9 2.5 %fusion.5 = bf16[2048,1024]{1,0:T(8,128)(2,1)} fusion(f32[32,64,1024]{2,1,0:T(8,128)S(1)} %get-tuple-element.10, f32[2048]{0:T(1024)S(1)} %subtract_multiply_fusion), kind=kLoop, calls=%fused_computation.7 | loop fusion | flops 4194304 | bytes 12591104 | tf_op jit(solution)/shard_map/convert_element_type | solution.py:37
  7.4 0.0 copy-start.3
  7.4 0.5 fusion.4
  7.9 0.0 copy-done
  7.9 1.7 copy-done.3
  9.6 4.6 %fusion = f32[2048,512]{0,1:S(1)} fusion(bf16[2048,512]{0,1:T(8,128)(2,1)S(1)} %bitcast.21, bf16[2048,1024]{1,0:T(8,128)(2,1)S(1)} %fusion.4, bf16[2048,1024]{1,0:T(8,128)(2,1)S(1)} %copy-done.3), kind=kOutput, calls=%fused_computation | convolution fusion | flops 4311744512 | bytes 14680064
  14.2 0.3 convert_element_type.29
  14.5 2.8 %reshape.51 = bf16[2,1024,512]{1,0,2:T(2,128)(2,1)} reshape(bf16[2048,8,64]{0,2,1:T(8,128)(2,1)S(1)} %convert_element_type.29) | data formatting | bytes 4194304 | tf_op jit(solution)/shard_map/reshape | solution.py:251
  17.2 8.3 %copy.7 = bf16[2,1024,512]{2,0,1:T(2,128)(2,1)S(1)} copy(bf16[2,1024,512]{1,0,2:T(2,128)(2,1)} %reshape.51) | data formatting | bytes 4194304 | tf_op jit(solution)/shard_map/reshape | solution.py:251
  25.5 55.8 %all_to_all.15 = bf16[2,1024,512]{2,0,1:T(2,128)(2,1)S(1)} all-to-all(bf16[2,1024,512]{2,0,1:T(2,128)(2,1)S(1)} %copy.7), channel_id=1, replica_groups=mesh['freq'=16,'src'=2] {'freq','src'}, dimensions={1} | all-to-all | bytes 4194304 | tf_op jit(solution)/shard_map/all_to_all | solution.py:252
  81.4 0.3 copy.8
  81.7 1.2 copy.9
  82.9 3.6 %reshape.52 = bf16[2,32,16,2,8,64]{5,4,3,2,1,0:T(8,128)(2,1)} reshape(bf16[2,32,32,512]{3,2,1,0:T(8,128)(2,1)S(1)} %copy.9) | data formatting | bytes 4194304 | tf_op jit(solution)/shard_map/reshape | solution.py:255
  86.4 9.2 %copy.10 = bf16[2,32,16,8,2,64]{5,4,3,2,1,0:T(2,128)(2,1)} copy(bf16[2,32,16,8,2,64]{5,3,4,2,1,0:T(8,128)(2,1)} %bitcast.22) | data formatting | bytes 4194304 | tf_op jit(solution)/shard_map/transpose | solution.py:258
  95.7 0.0 copy-start.1
  95.7 7.9 %reshape.53.x_ref = bf16[2,32,128,128]{3,2,1,0:T(8,128)(2,1)} reshape(bf16[2,32,16,8,2,64]{5,4,3,2,1,0:T(2,128)(2,1)} %copy.10) | data formatting | bytes 4194304 | tf_op jit(solution)/shard_map/reshape | solution.py:258
  103.6 0.0 copy-start.2
  103.6 1.6 copy-done.2
  105.2 94.1 %shard_map.41 = (f32[2,64,64,128]{3,2,1,0:T(8,128)}, f32[64,128]{1,0:T(8,128)S(1)}) custom-call(bf16[2,32,128,128]{3,2,1,0:T(8,128)(2,1)S(1)} %copy-done.2, f32[2,64,128,128]{3,2,1,0:T(8,128)} %offset_ref.1), custom_call_target="tpu_custom_call" | custom-call | tf_op jit(solution)/shard_map/pallas_call | solution.py:260
  199.3 4.8 %copy.13 = f32[2,64,64,128]{3,2,1,0:T(8,128)} copy(f32[2,64,64,128]{3,2,1,0:T(8,128)} %get-tuple-element.18) | data formatting | bytes 8388608
  204.1 0.6 copy.14
  204.7 0.0 copy-done.1
  (2 shorter events, 0.0 us)
Async XLA Ops:
  0.6 7.3 %copy-start = (bf16[8,2048,64]{1,2,0:T(8,128)(2,1)S(1)}, bf16[8,2048,64]{1,2,0:T(8,128)(2,1)}, u32[]{:S(2)}) copy-start(bf16[8,2048,64]{1,2,0:T(8,128)(2,1)} %param.2) | copy-start | bytes 6291460
  7.4 2.2 %copy-start.3 = (bf16[2048,1024]{1,0:T(8,128)(2,1)S(1)}, bf16[2048,1024]{1,0:T(8,128)(2,1)}, u32[]{:S(2)}) copy-start(bf16[2048,1024]{1,0:T(8,128)(2,1)} %fusion.5) | copy-start | bytes 12582916
  95.7 109.0 %copy-start.1 = (bf16[8,2048,64]{1,2,0:T(8,128)(2,1)S(1)}, bf16[8,2048,64]{1,2,0:T(8,128)(2,1)}, u32[]{:S(2)}) copy-start(bf16[8,2048,64]{1,2,0:T(8,128)(2,1)} %param.2) | copy-start | bytes 6291460
  103.6 1.6 copy-start.2

commit v2 on v1

--- a/solution.py
+++ b/solution.py
@@ -12,31 +12,24 @@
 step_size = 0.3
 epsilon = 1e-06
 MESH = pl.DeviceIdType.MESH
-LOW_STEPS = 64
-
-
-def waves(count, stride, length):
+LOW_STEPS = 128
+GROUP_BINS = 128
+PAIR = 2
+
+
+def waves(bin_idx, count, stride, length):
     index = jnp.arange(count, dtype=jnp.int32) * stride
-    bin_idx = jnp.arange(length // 2, dtype=jnp.int32)
-    phase = (index[:, None] * bin_idx[None, :] % length).astype(jnp.float32) * (
+    phase = (bin_idx[:, None] * index[None, :] % length).astype(jnp.float32) * (
         2.0 * jnp.pi / length
     )
-    return lax.optimization_barrier((jnp.cos(phase), jnp.sin(phase)))
-
-
-def dft_table(length):
-    high_cos, high_sin = waves(length // LOW_STEPS, LOW_STEPS, length)
-    low_cos, low_sin = waves(LOW_STEPS, 1, length)
+    return jnp.cos(phase), jnp.sin(phase)
+
+
+def window_of(length):
     sample_idx = jnp.arange(length, dtype=jnp.int32)
-    window = (
+    return (
         0.5 - 0.5 * jnp.cos(sample_idx.astype(jnp.float32) * (2.0 * jnp.pi / length))
     ) * jnp.sqrt(jnp.float32(8.0 / (3.0 * length)))
-    window = lax.optimization_barrier(window).reshape(-1, LOW_STEPS, 1)
-    a_cos, a_sin = high_cos[:, None, :], high_sin[:, None, :]
-    b_cos, b_sin = low_cos[None], low_sin[None]
-    cos_part = (window * (a_cos * b_cos - a_sin * b_sin)).astype(jnp.bfloat16)
-    sin_part = (-window * (a_sin * b_cos + a_cos * b_sin)).astype(jnp.bfloat16)
-    return jnp.concatenate([cos_part, sin_part], axis=2).reshape(length, length)
 
 
 def halves(value):
@@ -56,6 +49,102 @@
 def block_pair(real_imag, width):
     swapped = jnp.concatenate([-real_imag[:, width:], real_imag[:, :width]], axis=1)
     return jnp.concatenate([real_imag, swapped], axis=0)
+
+
+def spectra_kernel(
+    dims,
+    s_ref,
+    high_cos,
+    high_sin,
+    low_cos,
+    low_sin,
+    window,
+    out_ref,
+    table,
+    send_buf,
+    keep_sem,
+    send_sem,
+    recv_sem,
+):
+    freq_devices, src_devices = dims
+    devices = freq_devices * src_devices
+    my_freq, my_src = lax.axis_index("freq"), lax.axis_index("src")
+    slot = my_src * freq_devices + my_freq
+    bins = out_ref.shape[2]
+    length = s_ref.shape[1]
+    members = GROUP_BINS // bins
+    groups = devices // members
+
+    def place(index):
+        return (lax.rem(index, freq_devices), index // freq_devices)
+
+    barrier = pltpu.get_barrier_semaphore()
+
+    def greet(step, carry):
+        pl.semaphore_signal(
+            barrier, inc=1, device_id=place(lax.rem(slot + step, devices)), device_id_type=MESH
+        )
+        return carry
+
+    lax.fori_loop(1, devices, greet, 0)
+
+    def group_of(step):
+        return lax.rem(slot // members + step, groups)
+
+    def compute(step):
+        group = group_of(step)
+        rows = pl.ds(pl.multiple_of(group * GROUP_BINS, GROUP_BINS), GROUP_BINS)
+        l_cos, l_sin = low_cos[rows, :], low_sin[rows, :]
+        h_cos, h_sin = high_cos[rows, :], high_sin[rows, :]
+        for high in range(length // LOW_STEPS):
+            columns = slice(high * LOW_STEPS, (high + 1) * LOW_STEPS)
+            a_cos, a_sin = h_cos[:, high : high + 1], h_sin[:, high : high + 1]
+            weight = window[:, columns]
+            table[:GROUP_BINS, columns] = (weight * (a_cos * l_cos - a_sin * l_sin)).astype(
+                jnp.bfloat16
+            )
+            table[GROUP_BINS:, columns] = (-weight * (a_sin * l_cos + a_cos * l_sin)).astype(
+                jnp.bfloat16
+            )
+        y = dot_nt(table[...], s_ref[...]).astype(jnp.bfloat16)
+        for member in range(members):
+            owner = group * members + member
+            send_buf[owner, 0] = y[member * bins : (member + 1) * bins]
+            send_buf[owner, 1] = y[GROUP_BINS + member * bins : GROUP_BINS + (member + 1) * bins]
+
+    def send(step):
+        for member in range(members):
+            owner = group_of(step) * members + lax.rem(slot + member, members)
+
+            @pl.when(owner == slot)
+            def _():
+                pltpu.make_async_copy(send_buf.at[owner], out_ref.at[slot], keep_sem).start()
+
+            @pl.when(owner != slot)
+            def _():
+                pltpu.make_async_remote_copy(
+                    src_ref=send_buf.at[owner],
+                    dst_ref=out_ref.at[slot],
+                    send_sem=send_sem,
+                    recv_sem=recv_sem,
+                    device_id=place(owner),
+                    device_id_type=MESH,
+                ).start()
+
+    compute(0)
+    pl.semaphore_wait(barrier, devices - 1)
+    send(0)
+
+    def body(step, carry):
+        compute(step)
+        send(step)
+        return carry
+
+    lax.fori_loop(1, groups, body, 0)
+    pltpu.make_async_copy(send_buf.at[slot], out_ref.at[slot], keep_sem).wait()
+    others = out_ref.at[pl.ds(0, devices - 1)]
+    pltpu.make_async_copy(others, others, send_sem).wait()
+    pltpu.make_async_copy(others, others, recv_sem).wait()
 
 
 def demix_kernel(
@@ -78,11 +167,13 @@
     recv_sem,
     last_sem,
 ):
-    freq_devices, src_devices, total_bins = dims
+    freq_devices, src_devices, total_bins, frames_here = dims
     devices = freq_devices * src_devices
     my_freq, my_src = lax.axis_index("freq"), lax.axis_index("src")
     me = my_freq * src_devices + my_src
-    bins, frames, width = x_ref.shape[1], x_ref.shape[2], x_ref.shape[3]
+    bins = x_ref.shape[1]
+    width = offset_ref.shape[2]
+    frames = frames_here * freq_devices
     rows = width // src_devices
     chunk = width // devices
 
@@ -108,36 +199,61 @@
     col_id = lax.broadcasted_iota(jnp.int32, (width, 2 * width), 1)
     identity = jnp.where(row_id == col_id, 1.0, 0.0).astype(jnp.float32)
 
-    def separate(b, w):
-        high, low = halves(w)
-        product = dot_nt(jnp.concatenate([high, low], axis=0), x_buf[b])
-        y = (product[:width] + product[width:]).astype(jnp.bfloat16)
-        y_buf[b] = y
-        values = y.astype(jnp.float32)
-        squares = values * values
+    def separate(first_bin, w_list, x_list):
+        products = []
+        for w, x in zip(w_list, x_list):
+            high, low = halves(w)
+            products.append(dot_nt(jnp.concatenate([high, low], axis=0), x))
+        y_list = [(p[:width] + p[width:]).astype(jnp.bfloat16) for p in products]
+        squares = 0.0
+        for y in y_list:
+            values = y.astype(jnp.float32)
+            squares = squares + values * values
+        for k in range(PAIR):
+            w_buf[first_bin + k] = w_list[k]
+            y_buf[first_bin + k] = y_list[k]
         sums[...] += squares[:, :frames] + squares[:, frames:]
 
-    def first(b, carry):
-        w = jnp.concatenate([stage[0, b], stage[1, b]], axis=1) + identity
-        w_buf[b] = w
-        x_real, x_imag = x_ref[0, b], x_ref[1, b]
-        upper = jnp.concatenate([x_real, -x_imag], axis=1)
-        lower = jnp.concatenate([x_imag, x_real], axis=1)
-        x_buf[b] = jnp.concatenate([upper, lower], axis=0)
-        separate(b, w)
+    def gather_frames(part):
+        pieces = [part[k * freq_devices : (k + 1) * freq_devices] for k in range(src_devices)]
+        return jnp.concatenate(
+            [
+                jnp.concatenate([p[:, f * rows : (f + 1) * rows] for p in pieces], axis=1)
+                for f in range(frames_here)
+            ],
+            axis=0,
+        )
+
+    def first(step, carry):
+        b = step * PAIR
+        w_list, x_list = [], []
+        for k in range(PAIR):
+            w_list.append(jnp.concatenate([stage[0, b + k], stage[1, b + k]], axis=1) + identity)
+            x_real, x_imag = gather_frames(x_ref[0, b + k]), gather_frames(x_ref[1, b + k])
+            upper = jnp.concatenate([x_real, -x_imag], axis=1)
+            lower = jnp.concatenate([x_imag, x_real], axis=1)
+            x_list.append(jnp.concatenate([upper, lower], axis=0))
+        for k in range(PAIR):
+            x_buf[b + k] = x_list[k]
+        separate(b, w_list, x_list)
         return carry
 
-    def improved(b, scale):
-        y = y_buf[b]
-        high, low = halves(y.astype(jnp.float32) * scale)
-        product = dot_nt(jnp.concatenate([high, low], axis=0), block_pair(y, frames))
-        diff = identity - (product[:width] + product[width:])
-        d_high, d_low = halves(diff)
-        w = w_buf[b]
-        w_high, w_low = halves(w)
-        change = dot_nn(jnp.concatenate([d_high, d_low], axis=0), block_pair(w_high, width))
-        change_low = dot_nn(d_high, block_pair(w_low, width))
-        return w + step_size * (change[:width] + change[width:] + change_low)
+    def improved(first_bin, scale):
+        y_list = [y_buf[first_bin + k] for k in range(PAIR)]
+        w_list = [w_buf[first_bin + k] for k in range(PAIR)]
+        diffs = []
+        for y in y_list:
+            high, low = halves(y.astype(jnp.float32) * scale)
+            product = dot_nt(jnp.concatenate([high, low], axis=0), block_pair(y, frames))
+            diffs.append(identity - (product[:width] + product[width:]))
+        result = []
+        for diff, w in zip(diffs, w_list):
+            d_high, d_low = halves(diff)
+            w_high, w_low = halves(w)
+            change = dot_nn(jnp.concatenate([d_high, d_low], axis=0), block_pair(w_high, width))
+            change_low = dot_nn(d_high, block_pair(w_low, width))
+            result.append(w + step_size * (change[:width] + change[width:] + change_low))
+        return result
 
     def add_up(sweep):
         total = sums[...]
@@ -188,50 +304,58 @@
         return jnp.concatenate([inverse, inverse], axis=1)
 
     sums[...] = jnp.zeros_like(sums)
-    lax.fori_loop(0, bins, first, 0)
+    lax.fori_loop(0, bins // PAIR, first, 0)
     pl.semaphore_wait(barrier, devices - 1)
 
     for sweep in range(ITERS - 1):
         scale = add_up(sweep)
         sums[...] = jnp.zeros_like(sums)
 
-        def again(b, carry, scale=scale):
-            w = improved(b, scale)
-            w_buf[b] = w
-            separate(b, w)
+        def again(step, carry, scale=scale):
+            b = step * PAIR
+            x_list = [x_buf[b + k] for k in range(PAIR)]
+            separate(b, improved(b, scale), x_list)
             return carry
 
-        lax.fori_loop(0, bins, again, 0)
+        lax.fori_loop(0, bins // PAIR, again, 0)
 
     scale = add_up(ITERS - 1)
     power_ref[...] = power[pl.ds(pl.multiple_of(my_src * rows, rows), rows), :]
 
-    def last(b, carry):
-        w = improved(b, scale)
-        stage[0, b] = w[:, :width]
-        stage[1, b] = w[:, width:]
+    other = 1 - my_src
+    own_rows = pl.ds(pl.multiple_of(my_src * rows, rows), rows)
+    other_rows = pl.ds(pl.multiple_of(other * rows, rows), rows)
+
+    def keep_copy(start, count):
+        return pltpu.make_async_copy(
+            stage.at[:, pl.ds(start, count), own_rows],
+            out_ref.at[:, pl.ds(my_src * bins + start, count)],
+            load_sem,
+        )
+
+    def give_copy(start, count):
+        return pltpu.make_async_remote_copy(
+            src_ref=stage.at[:, pl.ds(start, count), other_rows],
+            dst_ref=out_ref.at[:, pl.ds(my_src * bins + start, count)],
+            send_sem=last_sem.at[0],
+            recv_sem=last_sem.at[1],
+            device_id=(my_freq, other),
+            device_id_type=MESH,
+        )
+
+    def last(step, carry):
+        b = step * PAIR
+        w_list = improved(b, scale)
+        for k in range(PAIR):
+            stage[0, b + k] = w_list[k][:, :width]
+            stage[1, b + k] = w_list[k][:, width:]
+        give_copy(b, PAIR).start()
+        keep_copy(b, PAIR).start()
         return carry
 
-    lax.fori_loop(0, bins, last, 0)
-    here = pl.ds(my_src * bins, bins)
-    keep = pltpu.make_async_copy(
-        stage.at[:, :, pl.ds(pl.multiple_of(my_src * rows, rows), rows)],
-        out_ref.at[:, here],
-        load_sem,
-    )
-    keep.start()
-    other = 1 - my_src
-    give = pltpu.make_async_remote_copy(
-        src_ref=stage.at[:, :, pl.ds(pl.multiple_of(other * rows, rows), rows)],
-        dst_ref=out_ref.at[:, here],
-        send_sem=last_sem.at[0],
-        recv_sem=last_sem.at[1],
-        device_id=(my_freq, other),
-        device_id_type=MESH,
-    )
-    give.start()
-    keep.wait()
-    give.wait()
+    lax.fori_loop(0, bins // PAIR, last, 0)
+    keep_copy(0, bins).wait()
+    give_copy(0, bins).wait()
 
 
 def shards(samples, initial_offset):
@@ -245,20 +369,37 @@
     width = initial_offset.shape[2]
     frame_total = frames_here * freq_devices
     chunk = width // devices
-    spectra = jnp.einsum(
-        "fnm,nc->cfm", samples, dft_table(length), preferred_element_type=jnp.float32
-    ).astype(jnp.bfloat16)
-    spectra = spectra.reshape(2, bin_count, frames_here * mics_here)
-    regrouped = lax.all_to_all(
-        spectra, ("freq", "src"), split_axis=1, concat_axis=2, tiled=True
+    f32, bf16 = jnp.float32, jnp.bfloat16
+    row = jnp.arange(bin_count, dtype=jnp.int32)
+    bin_idx = (
+        row // bins % freq_devices * pair_bins
+        + row // (bins * freq_devices) * bins
+        + row % bins
     )
-    regrouped = regrouped.reshape(
-        2, bins, freq_devices, src_devices, frames_here, mics_here
-    )
-    x = jnp.transpose(regrouped, (0, 1, 2, 4, 3, 5)).reshape(2, bins, frame_total, width)
-    f32, bf16 = jnp.float32, jnp.bfloat16
-    return pl.pallas_call(
-        functools.partial(demix_kernel, (freq_devices, src_devices, bin_count)),
+    high_cos, high_sin = waves(bin_idx, length // LOW_STEPS, LOW_STEPS, length)
+    low_cos, low_sin = waves(bin_idx, LOW_STEPS, 1, length)
+    columns = frames_here * mics_here
+    frames_of = jnp.transpose(samples, (0, 2, 1)).reshape(columns, length)
+    vmem = pl.BlockSpec(memory_space=pltpu.VMEM)
+    spectra = pl.pallas_call(
+        functools.partial(spectra_kernel, (freq_devices, src_devices)),
+        out_shape=jax.ShapeDtypeStruct((devices, 2, bins, columns), bf16),
+        in_specs=[vmem] * 6,
+        out_specs=vmem,
+        scratch_shapes=[
+            pltpu.VMEM((2 * GROUP_BINS, length), bf16),
+            pltpu.VMEM((devices, 2, bins, columns), bf16),
+            pltpu.SemaphoreType.DMA,
+            pltpu.SemaphoreType.DMA,
+            pltpu.SemaphoreType.DMA,
+        ],
+        compiler_params=pltpu.CompilerParams(
+            collective_id=1, has_side_effects=True, vmem_limit_bytes=40 * 1024 * 1024
+        ),
+    )(frames_of, high_cos, high_sin, low_cos, low_sin, window_of(length)[None])
+    x = jnp.transpose(spectra, (1, 2, 0, 3))
+    demixing, power = pl.pallas_call(
+        functools.partial(demix_kernel, (freq_devices, src_devices, bin_count, frames_here)),
         out_shape=(
             jax.ShapeDtypeStruct((2, pair_bins, width // src_devices, width), f32),
             jax.ShapeDtypeStruct((width // src_devices, frame_total), f32),
@@ -290,6 +431,8 @@
             collective_id=0, has_side_effects=True, vmem_limit_bytes=48 * 1024 * 1024
         ),
     )(x, initial_offset)
+    power = jnp.transpose(power.reshape(-1, frames_here, freq_devices), (0, 2, 1))
+    return demixing, power.reshape(-1, frame_total)
 
 
 def solution(mesh):

time: 205 us -> 133 us (0.65)
  blocking collectives: 55.8 us -> 0 us
  local copies, waits for them, and re-layouts: 42 us -> 6.96 us
  Pallas kernels: 94.1 us -> 121 us
  matrix products: 4.58 us -> 0 us
  other arithmetic: 7.53 us -> 4.33 us
    all_to_all x1 -> x0, blocking collectives: 55.8 us -> none  [shards(): lax.all_to_all(spectra, ('freq', 'src'), split_axis=1, concat_axis=2, til...]
    pallas_call x0 -> x1, Pallas kernels: none -> 49.4 us  [shards(): pl.pallas_call(functools.partial(spectra_kernel, (freq_devices, src_devic...]
    pallas_call x1, Pallas kernels: 94.1 us -> 71.5 us  [shards(): pl.pallas_call(functools.partial(demix_kernel, (freq_devices, src_devices...]
    reshape x4 -> x0, local copies, waits for them, and re-layouts: 22.6 us -> none  [the longest x2 11.1 us: shards(): spectra = spectra.reshape(2, bin_count, frames_here * mics_here)]
    transpose x1, local copies, waits for them, and re-layouts: 9.22 us -> 0.03 us  [shards(): jnp.transpose(power.reshape(-1, frames_here, freq_devices), (0, 2, 1))]
    unnamed x1 -> x0, matrix products: 4.58 us -> none
    convert_element_type x3 -> x1, other arithmetic: 3.35 us -> 0.1 us  [waves(): (bin_idx[:, None] * index[None, :] % length).astype(jnp.float32)]
    unnamed x10 -> x4, local copies, waits for them, and re-layouts: 8.66 us -> 5.49 us
where the time goes in v2:
time: 133 us
  Pallas kernels  121 us (91%)
  local copies, waits for them, and re-layouts  6.96 us (5%)
  other arithmetic  4.33 us (3%)
    pallas_call x1, Pallas kernels, shards(): pl.pallas_call(functools.partial(demix_kernel, (freq_devices, src_devices...  71.5 us
    pallas_call x1, Pallas kernels, shards(): pl.pallas_call(functools.partial(spectra_kernel, (freq_devices, src_devic...  49.4 us
    unnamed x4, local copies, waits for them, and re-layouts  5.49 us
    sin x2, other arithmetic, waves(): return (jnp.cos(phase), jnp.sin(phase))  3.98 us

profile of v2, /device:TPU:0, one launch (start us, length us, event | category | flops | bytes accessed | tf_op | source)
XLA Modules:
  0.0 132.8 jit_solution(2621250376667823095)
XLA Ops:
  0.6 0.0 copy-start
  0.7 0.2 subtract_multiply_fusion.window
  0.9 0.1 fusion.8
  1.0 0.2 copy.10
  1.2 1.9 %multiply_sine_fusion = (f32[1024,16]{1,0:T(8,128)S(1)}, f32[1024,16]{1,0:T(8,128)S(1)}) fusion(f32[1024,16]{1,0:T(8,128)S(1)} %copy.10), kind=kLoop, calls=%fused_computation.10 | loop fusion | flops 16384 | bytes 196608 | tf_op jit(solution)/shard_map/sin | solution.py:25
  3.1 2.1 %fusion.6 = (f32[1024,128]{1,0:T(8,128)S(1)}, f32[1024,128]{1,0:T(8,128)S(1)}) fusion(s32[1024]{0:T(1024)S(1)} %fusion.19), kind=kLoop, calls=%fused_computation.12 | loop fusion | flops 1835008 | bytes 1052672 | tf_op jit(solution)/shard_map/sin | solution.py:25
  5.2 0.0 copy-done
  5.2 49.4 %shard_map.41 = bf16[32,2,32,512]{3,2,1,0:T(8,128)(2,1)S(1)} custom-call(bf16[512,2048]{1,0:T(8,128)(2,1)S(1)} %bitcast.13, f32[1024,16]{1,0:T(8,128)S(1)} %get-tuple-element.11.high_cos, f32[1024,16]{1,0:T(8,128)S(1)} %get-tuple-element.10.high_sin, f32[1024,128]{1,0:T(8,128)S(1)} %get-tuple-element.13.low_cos, f32[1024,128]{1,0:T(8,128)S(1)} %get-tuple-element.12.low_sin, ...), custom_call_target="tpu_custom_call" | custom-call | tf_op jit(solution)/shard_map/pallas_call | solution.py:384
  54.6 1.2 copy.17
  55.7 71.5 %shard_map.42 = (f32[2,64,64,128]{3,2,1,0:T(8,128)}, f32[64,128]{1,0:T(8,128)S(1)}) custom-call(bf16[2,32,32,512]{3,2,1,0:T(8,128)(2,1)S(1)} %bitcast.12, f32[2,64,128,128]{3,2,1,0:T(8,128)} %offset_ref.1), custom_call_target="tpu_custom_call" | custom-call | tf_op jit(solution)/shard_map/pallas_call | solution.py:401
  127.2 0.1 copy.12
  127.3 0.7 copy.14
  128.0 4.8 %copy.20 = f32[2,64,64,128]{3,2,1,0:T(8,128)} copy(f32[2,64,64,128]{3,2,1,0:T(8,128)} %get-tuple-element.16) | data formatting | bytes 8388608
  (3 shorter events, 0.0 us)
Async XLA Ops:
  0.6 4.6 %copy-start = (bf16[8,2048,64]{1,2,0:T(8,128)(2,1)S(1)}, bf16[8,2048,64]{1,2,0:T(8,128)(2,1)}, u32[]{:S(2)}) copy-start(bf16[8,2048,64]{1,2,0:T(8,128)(2,1)} %param.2) | copy-start | bytes 6291460

commit v3 on v2

--- a/solution.py
+++ b/solution.py
@@ -14,7 +14,7 @@
 MESH = pl.DeviceIdType.MESH
 LOW_STEPS = 128
 GROUP_BINS = 128
-PAIR = 2
+PAIR = 8
 
 
 def waves(bin_idx, count, stride, length):

time: 133 us -> 116 us (0.87)
  Pallas kernels: 121 us -> 104 us
    pallas_call x1, Pallas kernels: 71.5 us -> 54.7 us  [shards(): pl.pallas_call(functools.partial(demix_kernel, (freq_devices, src_devices...]
where the time goes in v3:
time: 116 us
  Pallas kernels  104 us (90%)
  local copies, waits for them, and re-layouts  6.96 us (6%)
  other arithmetic  4.33 us (4%)
    pallas_call x1, Pallas kernels, shards(): pl.pallas_call(functools.partial(demix_kernel, (freq_devices, src_devices...  54.7 us
    pallas_call x1, Pallas kernels, shards(): pl.pallas_call(functools.partial(spectra_kernel, (freq_devices, src_devic...  49.4 us
    unnamed x4, local copies, waits for them, and re-layouts  5.49 us
    sin x2, other arithmetic, waves(): return (jnp.cos(phase), jnp.sin(phase))  3.98 us

profile of v3, /device:TPU:0, one launch (start us, length us, event | category | flops | bytes accessed | tf_op | source)
XLA Modules:
  0.0 116.1 jit_solution(2611628759817694572)
XLA Ops:
  0.6 0.0 copy-start
  0.7 0.2 subtract_multiply_fusion.window
  0.9 0.1 fusion.8
  1.0 0.2 copy.10
  1.2 1.9 %multiply_sine_fusion = (f32[1024,16]{1,0:T(8,128)S(1)}, f32[1024,16]{1,0:T(8,128)S(1)}) fusion(f32[1024,16]{1,0:T(8,128)S(1)} %copy.10), kind=kLoop, calls=%fused_computation.10 | loop fusion | flops 16384 | bytes 196608 | tf_op jit(solution)/shard_map/sin | solution.py:25
  3.1 2.1 %fusion.6 = (f32[1024,128]{1,0:T(8,128)S(1)}, f32[1024,128]{1,0:T(8,128)S(1)}) fusion(s32[1024]{0:T(1024)S(1)} %fusion.19), kind=kLoop, calls=%fused_computation.12 | loop fusion | flops 1835008 | bytes 1052672 | tf_op jit(solution)/shard_map/sin | solution.py:25
  5.2 0.0 copy-done
  5.2 49.4 %shard_map.41 = bf16[32,2,32,512]{3,2,1,0:T(8,128)(2,1)S(1)} custom-call(bf16[512,2048]{1,0:T(8,128)(2,1)S(1)} %bitcast.13, f32[1024,16]{1,0:T(8,128)S(1)} %get-tuple-element.11.high_cos, f32[1024,16]{1,0:T(8,128)S(1)} %get-tuple-element.10.high_sin, f32[1024,128]{1,0:T(8,128)S(1)} %get-tuple-element.13.low_cos, f32[1024,128]{1,0:T(8,128)S(1)} %get-tuple-element.12.low_sin, ...), custom_call_target="tpu_custom_call" | custom-call | tf_op jit(solution)/shard_map/pallas_call | solution.py:384
  54.6 1.2 %copy.17 = bf16[32,2,32,512]{3,0,2,1:T(8,128)(2,1)S(1)} copy(bf16[32,2,32,512]{3,2,1,0:T(8,128)(2,1)S(1)} %shard_map.41) | data formatting | bytes 4194304 | tf_op jit(solution)/shard_map/pallas_call | solution.py:384
  55.7 54.7 %shard_map.42 = (f32[2,64,64,128]{3,2,1,0:T(8,128)}, f32[64,128]{1,0:T(8,128)S(1)}) custom-call(bf16[2,32,32,512]{3,2,1,0:T(8,128)(2,1)S(1)} %bitcast.12, f32[2,64,128,128]{3,2,1,0:T(8,128)} %offset_ref.1), custom_call_target="tpu_custom_call" | custom-call | tf_op jit(solution)/shard_map/pallas_call | solution.py:401
  110.5 0.1 copy.12
  110.6 0.7 copy.14
  111.3 4.8 %copy.20 = f32[2,64,64,128]{3,2,1,0:T(8,128)} copy(f32[2,64,64,128]{3,2,1,0:T(8,128)} %get-tuple-element.16) | data formatting | bytes 8388608
  (3 shorter events, 0.0 us)
Async XLA Ops:
  0.6 4.6 %copy-start = (bf16[8,2048,64]{1,2,0:T(8,128)(2,1)S(1)}, bf16[8,2048,64]{1,2,0:T(8,128)(2,1)}, u32[]{:S(2)}) copy-start(bf16[8,2048,64]{1,2,0:T(8,128)(2,1)} %param.2) | copy-start | bytes 6291460

commit v4 on v3

--- a/solution.py
+++ b/solution.py
@@ -17,9 +17,8 @@
 PAIR = 8
 
 
-def waves(bin_idx, count, stride, length):
-    index = jnp.arange(count, dtype=jnp.int32) * stride
-    phase = (bin_idx[:, None] * index[None, :] % length).astype(jnp.float32) * (
+def waves(bin_idx, index, length):
+    phase = (bin_idx * index % length).astype(jnp.float32) * (
         2.0 * jnp.pi / length
     )
     return jnp.cos(phase), jnp.sin(phase)
@@ -89,13 +88,13 @@
     lax.fori_loop(1, devices, greet, 0)
 
     def group_of(step):
-        return lax.rem(slot // members + step, groups)
+        return lax.rem(slot // members + step + groups // 4, groups)
 
     def compute(step):
         group = group_of(step)
         rows = pl.ds(pl.multiple_of(group * GROUP_BINS, GROUP_BINS), GROUP_BINS)
         l_cos, l_sin = low_cos[rows, :], low_sin[rows, :]
-        h_cos, h_sin = high_cos[rows, :], high_sin[rows, :]
+        h_cos, h_sin = high_cos[:, rows].T, high_sin[:, rows].T
         for high in range(length // LOW_STEPS):
             columns = slice(high * LOW_STEPS, (high + 1) * LOW_STEPS)
             a_cos, a_sin = h_cos[:, high : high + 1], h_sin[:, high : high + 1]
@@ -376,8 +375,10 @@
         + row // (bins * freq_devices) * bins
         + row % bins
     )
-    high_cos, high_sin = waves(bin_idx, length // LOW_STEPS, LOW_STEPS, length)
-    low_cos, low_sin = waves(bin_idx, LOW_STEPS, 1, length)
+    high = jnp.arange(length // LOW_STEPS, dtype=jnp.int32) * LOW_STEPS
+    low = jnp.arange(LOW_STEPS, dtype=jnp.int32)
+    high_cos, high_sin = waves(bin_idx[None, :], high[:, None], length)
+    low_cos, low_sin = waves(bin_idx[:, None], low[None, :], length)
     columns = frames_here * mics_here
     frames_of = jnp.transpose(samples, (0, 2, 1)).reshape(columns, length)
     vmem = pl.BlockSpec(memory_space=pltpu.VMEM)

time: 116 us -> 114 us (0.983)
  other arithmetic: 4.33 us -> 2.69 us
  local copies, waits for them, and re-layouts: 6.96 us -> 8.36 us
    unnamed x4, local copies, waits for them, and re-layouts: 5.49 us -> 7.07 us
    sin x2, other arithmetic: 3.98 us -> 2.44 us  [waves(): return (jnp.cos(phase), jnp.sin(phase))]
    pallas_call x1, Pallas kernels: 49.4 us -> 48 us  [shards(): pl.pallas_call(functools.partial(spectra_kernel, (freq_devices, src_devic...]
where the time goes in v4:
time: 114 us
  Pallas kernels  103 us (90%)
  local copies, waits for them, and re-layouts  8.36 us (7%)
  other arithmetic  2.69 us (2%)
    pallas_call x1, Pallas kernels, shards(): pl.pallas_call(functools.partial(demix_kernel, (freq_devices, src_devices...  54.5 us
    pallas_call x1, Pallas kernels, shards(): pl.pallas_call(functools.partial(spectra_kernel, (freq_devices, src_devic...  48 us
    unnamed x4, local copies, waits for them, and re-layouts  7.07 us
    sin x2, other arithmetic, waves(): return (jnp.cos(phase), jnp.sin(phase))  2.44 us

profile of v4, /device:TPU:0, one launch (start us, length us, event | category | flops | bytes accessed | tf_op | source)
XLA Modules:
  0.0 114.3 jit_solution(15002204007292283031)
XLA Ops:
  0.7 0.2 subtract_multiply_fusion.window
  0.9 0.3 fusion.11
  1.2 2.1 %fusion.6 = (f32[1024,128]{1,0:T(8,128)S(1)}, f32[1024,128]{1,0:T(8,128)S(1)}) fusion(s32[1024]{0:T(1024)S(1)} %fusion.22), kind=kLoop, calls=%fused_computation.10 | loop fusion | flops 1835008 | bytes 1052672 | tf_op jit(solution)/shard_map/sin | solution.py:24
  3.3 0.0 copy-start
  3.4 1.6 %copy-done = bf16[8,2048,64]{1,2,0:T(8,128)(2,1)S(1)} copy-done((bf16[8,2048,64]{1,2,0:T(8,128)(2,1)S(1)}, bf16[8,2048,64]{1,2,0:T(8,128)(2,1)}, u32[]{:S(2)}) %copy-start) | copy-done | bytes 2097176
  4.9 48.0 %shard_map.41 = bf16[32,2,32,512]{3,2,1,0:T(8,128)(2,1)S(1)} custom-call(bf16[512,2048]{1,0:T(8,128)(2,1)S(1)} %bitcast.13, f32[16,1024]{1,0:T(8,128)S(1)} %get-tuple-element.9.high_cos, f32[16,1024]{1,0:T(8,128)S(1)} %get-tuple-element.8.high_sin, f32[1024,128]{1,0:T(8,128)S(1)} %get-tuple-element.11.low_cos, f32[1024,128]{1,0:T(8,128)S(1)} %get-tuple-element.10.low_sin, ...), custom_call_target="tpu_custom_call" | custom-call | tf_op jit(solution)/shard_map/pallas_call | solution.py:385
  53.0 1.2 %copy.12 = bf16[32,2,32,512]{3,0,2,1:T(8,128)(2,1)S(1)} copy(bf16[32,2,32,512]{3,2,1,0:T(8,128)(2,1)S(1)} %shard_map.41) | data formatting | bytes 4194304 | tf_op jit(solution)/shard_map/pallas_call | solution.py:385
  54.1 54.5 %shard_map.42 = (f32[2,64,64,128]{3,2,1,0:T(8,128)}, f32[64,128]{1,0:T(8,128)S(1)}) custom-call(bf16[2,32,32,512]{3,2,1,0:T(8,128)(2,1)S(1)} %bitcast.12, f32[2,64,128,128]{3,2,1,0:T(8,128)} %offset_ref.1), custom_call_target="tpu_custom_call" | custom-call | tf_op jit(solution)/shard_map/pallas_call | solution.py:402
  108.6 0.1 copy.7
  108.8 0.7 copy.9
  109.5 4.8 %copy.15 = f32[2,64,64,128]{3,2,1,0:T(8,128)} copy(f32[2,64,64,128]{3,2,1,0:T(8,128)} %get-tuple-element.14) | data formatting | bytes 8388608
  (3 shorter events, 0.0 us)
Async XLA Ops:
  3.3 1.6 %copy-start = (bf16[8,2048,64]{1,2,0:T(8,128)(2,1)S(1)}, bf16[8,2048,64]{1,2,0:T(8,128)(2,1)}, u32[]{:S(2)}) copy-start(bf16[8,2048,64]{1,2,0:T(8,128)(2,1)} %param.2) | copy-start | bytes 6291460

commit v5 on v4

--- a/solution.py
+++ b/solution.py
@@ -14,7 +14,7 @@
 MESH = pl.DeviceIdType.MESH
 LOW_STEPS = 128
 GROUP_BINS = 128
-PAIR = 8
+BATCH = 16
 
 
 def waves(bin_idx, index, length):
@@ -174,6 +174,7 @@
     width = offset_ref.shape[2]
     frames = frames_here * freq_devices
     rows = width // src_devices
+    batch = min(BATCH, bins)
     chunk = width // devices
 
     def place(index):
@@ -208,7 +209,7 @@
         for y in y_list:
             values = y.astype(jnp.float32)
             squares = squares + values * values
-        for k in range(PAIR):
+        for k in range(batch):
             w_buf[first_bin + k] = w_list[k]
             y_buf[first_bin + k] = y_list[k]
         sums[...] += squares[:, :frames] + squares[:, frames:]
@@ -224,22 +225,22 @@
         )
 
     def first(step, carry):
-        b = step * PAIR
+        b = step * batch
         w_list, x_list = [], []
-        for k in range(PAIR):
+        for k in range(batch):
             w_list.append(jnp.concatenate([stage[0, b + k], stage[1, b + k]], axis=1) + identity)
             x_real, x_imag = gather_frames(x_ref[0, b + k]), gather_frames(x_ref[1, b + k])
             upper = jnp.concatenate([x_real, -x_imag], axis=1)
             lower = jnp.concatenate([x_imag, x_real], axis=1)
             x_list.append(jnp.concatenate([upper, lower], axis=0))
-        for k in range(PAIR):
+        for k in range(batch):
             x_buf[b + k] = x_list[k]
         separate(b, w_list, x_list)
         return carry
 
     def improved(first_bin, scale):
-        y_list = [y_buf[first_bin + k] for k in range(PAIR)]
-        w_list = [w_buf[first_bin + k] for k in range(PAIR)]
+        y_list = [y_buf[first_bin + k] for k in range(batch)]
+        w_list = [w_buf[first_bin + k] for k in range(batch)]
         diffs = []
         for y in y_list:
             high, low = halves(y.astype(jnp.float32) * scale)
@@ -303,7 +304,7 @@
         return jnp.concatenate([inverse, inverse], axis=1)
 
     sums[...] = jnp.zeros_like(sums)
-    lax.fori_loop(0, bins // PAIR, first, 0)
+    lax.fori_loop(0, bins // batch, first, 0)
     pl.semaphore_wait(barrier, devices - 1)
 
     for sweep in range(ITERS - 1):
@@ -311,12 +312,12 @@
         sums[...] = jnp.zeros_like(sums)
 
         def again(step, carry, scale=scale):
-            b = step * PAIR
-            x_list = [x_buf[b + k] for k in range(PAIR)]
+            b = step * batch
+            x_list = [x_buf[b + k] for k in range(batch)]
             separate(b, improved(b, scale), x_list)
             return carry
 
-        lax.fori_loop(0, bins // PAIR, again, 0)
+        lax.fori_loop(0, bins // batch, again, 0)
 
     scale = add_up(ITERS - 1)
     power_ref[...] = power[pl.ds(pl.multiple_of(my_src * rows, rows), rows), :]
@@ -343,16 +344,16 @@
         )
 
     def last(step, carry):
-        b = step * PAIR
+        b = step * batch
         w_list = improved(b, scale)
-        for k in range(PAIR):
+        for k in range(batch):
             stage[0, b + k] = w_list[k][:, :width]
             stage[1, b + k] = w_list[k][:, width:]
-        give_copy(b, PAIR).start()
-        keep_copy(b, PAIR).start()
+        give_copy(b, batch).start()
+        keep_copy(b, batch).start()
         return carry
 
-    lax.fori_loop(0, bins // PAIR, last, 0)
+    lax.fori_loop(0, bins // batch, last, 0)
     keep_copy(0, bins).wait()
     give_copy(0, bins).wait()
 

time: 114 us -> 113 us (level)
  Pallas kernels: 103 us -> 101 us
    pallas_call x1, Pallas kernels: 54.5 us -> 52.9 us  [shards(): pl.pallas_call(functools.partial(demix_kernel, (freq_devices, src_devices...]
where the time goes in v5:
time: 113 us
  Pallas kernels  101 us (89%)
  local copies, waits for them, and re-layouts  8.36 us (7%)
  other arithmetic  2.69 us (2%)
    pallas_call x1, Pallas kernels, shards(): pl.pallas_call(functools.partial(demix_kernel, (freq_devices, src_devices...  52.9 us
    pallas_call x1, Pallas kernels, shards(): pl.pallas_call(functools.partial(spectra_kernel, (freq_devices, src_devic...  48 us
    unnamed x4, local copies, waits for them, and re-layouts  7.07 us
    sin x2, other arithmetic, waves(): return (jnp.cos(phase), jnp.sin(phase))  2.44 us

profile of v5, /device:TPU:0, one launch (start us, length us, event | category | flops | bytes accessed | tf_op | source)
XLA Modules:
  0.0 112.7 jit_solution(9175422669403273189)
XLA Ops:
  0.7 0.2 subtract_multiply_fusion.window
  0.9 0.3 fusion.11
  1.2 2.1 %fusion.6 = (f32[1024,128]{1,0:T(8,128)S(1)}, f32[1024,128]{1,0:T(8,128)S(1)}) fusion(s32[1024]{0:T(1024)S(1)} %fusion.22), kind=kLoop, calls=%fused_computation.10 | loop fusion | flops 1835008 | bytes 1052672 | tf_op jit(solution)/shard_map/sin | solution.py:24
  3.3 0.0 copy-start
  3.4 1.6 %copy-done = bf16[8,2048,64]{1,2,0:T(8,128)(2,1)S(1)} copy-done((bf16[8,2048,64]{1,2,0:T(8,128)(2,1)S(1)}, bf16[8,2048,64]{1,2,0:T(8,128)(2,1)}, u32[]{:S(2)}) %copy-start) | copy-done | bytes 2097176
  4.9 48.0 %shard_map.41 = bf16[32,2,32,512]{3,2,1,0:T(8,128)(2,1)S(1)} custom-call(bf16[512,2048]{1,0:T(8,128)(2,1)S(1)} %bitcast.13, f32[16,1024]{1,0:T(8,128)S(1)} %get-tuple-element.9.high_cos, f32[16,1024]{1,0:T(8,128)S(1)} %get-tuple-element.8.high_sin, f32[1024,128]{1,0:T(8,128)S(1)} %get-tuple-element.11.low_cos, f32[1024,128]{1,0:T(8,128)S(1)} %get-tuple-element.10.low_sin, ...), custom_call_target="tpu_custom_call" | custom-call | tf_op jit(solution)/shard_map/pallas_call | solution.py:386
  53.0 1.2 %copy.12 = bf16[32,2,32,512]{3,0,2,1:T(8,128)(2,1)S(1)} copy(bf16[32,2,32,512]{3,2,1,0:T(8,128)(2,1)S(1)} %shard_map.41) | data formatting | bytes 4194304 | tf_op jit(solution)/shard_map/pallas_call | solution.py:386
  54.1 52.9 %shard_map.42 = (f32[2,64,64,128]{3,2,1,0:T(8,128)}, f32[64,128]{1,0:T(8,128)S(1)}) custom-call(bf16[2,32,32,512]{3,2,1,0:T(8,128)(2,1)S(1)} %bitcast.12, f32[2,64,128,128]{3,2,1,0:T(8,128)} %offset_ref.1), custom_call_target="tpu_custom_call" | custom-call | tf_op jit(solution)/shard_map/pallas_call | solution.py:403
  107.1 0.1 copy.7
  107.2 0.7 copy.9
  107.9 4.8 %copy.15 = f32[2,64,64,128]{3,2,1,0:T(8,128)} copy(f32[2,64,64,128]{3,2,1,0:T(8,128)} %get-tuple-element.14) | data formatting | bytes 8388608
  (3 shorter events, 0.0 us)
Async XLA Ops:
  3.3 1.6 %copy-start = (bf16[8,2048,64]{1,2,0:T(8,128)(2,1)S(1)}, bf16[8,2048,64]{1,2,0:T(8,128)(2,1)}, u32[]{:S(2)}) copy-start(bf16[8,2048,64]{1,2,0:T(8,128)(2,1)} %param.2) | copy-start | bytes 6291460
